TPU v7x, 256 devices: a whole 4x4x8 slice. The times are simulated.
256 devices in a mesh: dp: 128 (over x, y, z), group: 2 (over core).
Axes of the slice: x: 4, y: 4, z: 8, core: 2. Of those that a mesh axis runs over, the one named last changes fastest.
Arguments:
- tokens_in: bfloat16 [128, 256, 1536], P('dp', None, 'group'), may hold values from -24 to 24
- dw_kernel: float32 [7, 1536], P(None, 'group'), may hold values from -2 to 2
- point_weight: bfloat16 [1536, 1536], P(None, 'group'), may hold values from -0.15625 to 0.15625
- positive_emb: bfloat16 [128, 1536], P('dp', 'group'), may hold values from -0.15625 to 0.15625
- bank: bfloat16 [16384, 1536], P('dp', 'group'), may hold values from -0.15625 to 0.15625
- neg_owner: int32 [16384, 1], P('dp'), may hold values from 0 to 127; in each aligned block of 128 rows (0 to 127, 128 to 255, ...) at most 2 rows name the same one
- neg_block: int32 [16384], P('dp'), may hold values from 0 to 15
Outputs:
- grad_bank: float32 [16384, 1536], P('dp', 'group')
- grad_kernel: float32 [7, 1536], P(None, 'group')
- grad_weight: float32 [1536, 1536], P('dp', 'group')
Inputs may be any that keep to these rules, and one draw needn't show every extreme that they name: `neg_owner`: among the 128 requests of one batch shard (aligned blocks of 128 rows), no owner is named more than 2 times.
All inputs are finite; a program needn't handle non-finite values.
Results may differ from a plain program's by a relative error of at most 0.0036.
Values may be sent and summed in bfloat16 or wider, within the bound.
No kernel may reach another device: no remote copies, remote signals or barrier semaphores. Data moves between devices by JAX's collectives and lax.ppermute only.
A program may use at most 128 MiB of HBM per device.

v0:
```python
import jax
import jax.numpy as jnp
from jax import lax
from jax.sharding import PartitionSpec as P

ROWS = 8
CAP = 2
SOFTMAX_TEMPER = 0.07
LOSS_SCALE = 256.0
EPSILON = 1e-06
PRECISE = lax.Precision.HIGHEST


def depthwise(tokens, kernel):
    margin = kernel.shape[0] // 2
    seq_length = tokens.shape[1]
    padded = jnp.pad(tokens.astype(jnp.float32), ((0, 0), (margin, margin), (0, 0)))
    running_sum = jnp.zeros(tokens.shape, jnp.float32)
    for tap_index in range(kernel.shape[0]):
        running_sum = (
            running_sum + kernel[tap_index] * padded[:, tap_index : tap_index + seq_length, :]
        )
    return (running_sum, padded)


def kernel_term(grad_hidden, padded, tap_count):
    seq_length = grad_hidden.shape[1]
    return jnp.stack(
        [
            jnp.sum(grad_hidden * padded[:, tap_index : tap_index + seq_length, :], axis=(0, 1))
            for tap_index in range(tap_count)
        ]
    )


def gelu_back(mixed_out, cotangent):
    return jax.vjp(lambda entry_value: jax.nn.gelu(entry_value, approximate=True), mixed_out)[1](
        cotangent
    )[0]


def per_device(tokens_in, dw_kernel, point_weight, positive_emb, bank, neg_owner, neg_block):
    seq_count, seq_length, half_width = tokens_in.shape
    token_count = seq_count * seq_length
    device_count = lax.axis_size("dp")
    slot_count = device_count * CAP
    block_count = bank.shape[0] // ROWS
    request_count = neg_owner.shape[0]
    local_rows = bank.shape[0]
    local_end = seq_count + local_rows
    hidden_f, padded = depthwise(tokens_in, dw_kernel)
    hidden = hidden_f.astype(jnp.bfloat16).reshape(token_count, half_width)
    mixed_part = lax.dot_general(
        hidden, point_weight, (((1,), (1,)), ((), ())), preferred_element_type=jnp.float32
    )
    mixed_out = lax.psum_scatter(mixed_part, "group", scatter_dimension=1, tiled=True)
    activated = jax.nn.gelu(mixed_out, approximate=True)
    embedding = jnp.mean(
        tokens_in.astype(jnp.float32) + activated.reshape(seq_count, seq_length, half_width), axis=1
    )
    owners = neg_owner[:, 0]
    owner_hits = (owners[:, None] == jnp.arange(device_count, dtype=jnp.int32)[None, :]).astype(
        jnp.int32
    )
    earlier = jnp.cumsum(owner_hits, axis=0) - owner_hits
    rank_in_owner = jnp.sum(earlier * owner_hits, axis=1)
    slot_index = owners * CAP + rank_in_owner
    slot_hits = (slot_index[:, None] == jnp.arange(slot_count, dtype=jnp.int32)[None, :]).astype(
        jnp.int32
    )
    wanted = jnp.sum(slot_hits * (neg_block[:, None] + 1), axis=0) - 1
    asked_blocks = lax.all_to_all(
        wanted.reshape(device_count, CAP), "dp", split_axis=0, concat_axis=0, tiled=True
    )
    asked_flat = asked_blocks.reshape(slot_count)
    blocks_local = bank.reshape(block_count, ROWS, half_width)
    served = jnp.take(blocks_local, jnp.maximum(asked_flat, 0), axis=0)
    served = jnp.where((asked_flat >= 0)[:, None, None], served, jnp.zeros((), jnp.bfloat16))
    fetched = lax.all_to_all(
        served.reshape(device_count, CAP, ROWS, half_width),
        "dp",
        split_axis=0,
        concat_axis=0,
        tiled=True,
    )
    negatives = jnp.take(fetched.reshape(slot_count, ROWS, half_width), slot_index, axis=0).reshape(
        request_count * ROWS, half_width
    )
    key_rows = jnp.concatenate([positive_emb, bank, negatives], axis=0)
    column_count = key_rows.shape[0]
    key_float = key_rows.astype(jnp.float32)
    dots_part = lax.dot_general(embedding, key_float, (((1,), (1,)), ((), ())), precision=PRECISE)
    inner_products, embed_sq, key_sq = lax.psum(
        (dots_part, jnp.sum(embedding * embedding, axis=1), jnp.sum(key_float * key_float, axis=1)),
        "group",
    )
    embedding_norm = jnp.sqrt(embed_sq + EPSILON)
    key_length_norm = jnp.sqrt(key_sq + EPSILON)
    score_matrix = inner_products / (
        SOFTMAX_TEMPER * embedding_norm[:, None] * key_length_norm[None, :]
    )
    exponent = jnp.exp(score_matrix)
    weights = exponent / jnp.sum(exponent, axis=1, keepdims=True)
    score_gradient = LOSS_SCALE * (weights - jnp.eye(seq_count, column_count, dtype=jnp.float32))
    blend_factor = score_gradient / (SOFTMAX_TEMPER * key_length_norm[None, :])
    unit_query = embedding / embedding_norm[:, None]
    row_weight = jnp.sum(score_gradient * score_matrix, axis=1)
    column_weight = jnp.sum(score_gradient * score_matrix, axis=0)
    key_scale = column_weight / (key_length_norm * key_length_norm)
    query_dir = jnp.dot(blend_factor, key_float, precision=PRECISE)
    embed_grad = (query_dir - row_weight[:, None] * unit_query) / embedding_norm[:, None]
    key_grad = (
        lax.dot_general(blend_factor, unit_query, (((0,), (0,)), ((), ())), precision=PRECISE)
        - key_scale[:, None] * key_float
    )
    local_grad = key_grad[seq_count:local_end]
    neg_grad = key_grad[local_end:].reshape(request_count, ROWS, half_width)
    outgoing = jnp.zeros((slot_count, ROWS, half_width), jnp.float32).at[slot_index].set(neg_grad)
    returned = lax.all_to_all(
        outgoing.reshape(device_count, CAP, ROWS, half_width),
        "dp",
        split_axis=0,
        concat_axis=0,
        tiled=True,
    )
    block_pick = (asked_flat[:, None] == jnp.arange(block_count, dtype=jnp.int32)[None, :]).astype(
        jnp.float32
    )
    remote = lax.dot_general(
        block_pick,
        returned.reshape(slot_count, ROWS * half_width),
        (((0,), (0,)), ((), ())),
        precision=PRECISE,
    )
    bank_grad = local_grad + remote.reshape(local_rows, half_width)
    act_grad = jnp.broadcast_to(
        (embed_grad / seq_length)[:, None, :], (seq_count, seq_length, half_width)
    ).reshape(token_count, half_width)
    mixed_grad = gelu_back(mixed_out, act_grad).astype(jnp.bfloat16)
    mixed_all = lax.all_gather(mixed_grad, "group", axis=1, tiled=True)
    hidden_grad = jnp.dot(mixed_all, point_weight, preferred_element_type=jnp.float32)
    kernel_part = kernel_term(
        hidden_grad.reshape(seq_count, seq_length, half_width), padded, dw_kernel.shape[0]
    )
    kernel_grad = lax.psum(kernel_part, "dp") / device_count
    weight_grad = (
        lax.psum_scatter(
            lax.dot_general(
                mixed_all, hidden, (((0,), (0,)), ((), ())), preferred_element_type=jnp.float32
            ),
            "dp",
            scatter_dimension=0,
            tiled=True,
        )
        / device_count
    )
    return (bank_grad, kernel_grad, weight_grad)


def solution(mesh):
    in_specs = (
        P("dp", None, "group"),
        P(None, "group"),
        P(None, "group"),
        P("dp", "group"),
        P("dp", "group"),
        P("dp", None),
        P("dp"),
    )
    out_specs = (P("dp", "group"), P(None, "group"), P("dp", "group"))
    return jax.shard_map(
        per_device, mesh=mesh, in_specs=in_specs, out_specs=out_specs, check_vma=False
    )
```

profile of v0, /device:TPU:54, one launch (start us, length us, event | category | flops | bytes accessed | tf_op | source)
XLA Modules:
  0.0 1563.4 jit_solution(61074231811996590)
XLA Ops:
  10.7 22.3 %all_to_all.16 = s32[128,1,2]{2,1,0:T(1,128)S(1)} all-to-all(s32[128,1,2]{2,1,0:T(1,128)S(1)} %bitcast.66), channel_id=1, replica_groups=mesh['dp'=128,'group'=2] {'dp'}, dimensions={0} | all-to-all | bytes 2048 | tf_op jit(solution)/shard_map/all_to_all | solution.py:72
  33.6 3.4 gather_fusion
  37.0 3.5 select_select_fusion
  40.5 11.9 all-to-all-start.1
  54.1 2.0 fusion.14
  56.3 15.2 reduce-scatter.4.cloned.1.call-done
  71.4 1.5 fusion.10
  73.5 48.7 %all-to-all-done.1 = bf16[128,2,8,768]{3,2,1,0:T(8,128)(2,1)} async-done(((bf16[128,2,8,768]{3,2,1,0:T(8,128)(2,1)}), bf16[128,2,8,768]{3,2,1,0:T(8,128)(2,1)}, u32[]{:S(2)}, u32[]{:S(2)}) %all-to-all-start.1) | async-done | bytes 3145760 | tf_op jit(solution)/shard_map/all_to_all | solution.py:79
  122.2 3.7 gather_fusion.1
  126.0 2.8 bitcast_select_fusion
  128.8 10.8 concatenate.3
  139.6 1.9 fusion.1
  141.5 3.0 fusion.27
  144.5 4.5 all-reduce.3
  151.7 2.3 convolution_reduce_fusion
  155.3 1.7 copy-done.3
  157.0 1.9 slice_bitcast_fusion
  158.9 3.1 broadcast_in_dim.66
  161.9 18.4 %scatter_fusion = f32[256,8,768]{2,1,0:T(8,128)} fusion(f32[256,8,768]{2,1,0:T(8,128)} %broadcast_in_dim.66, s32[128]{0:T(128)S(1)} %get-tuple-element.37, f32[128,8,768]{2,1,0:T(8,128)} %slice_bitcast_fusion), kind=kCustom, calls=%fused_computation.2 | custom fusion | bytes 9437696 | tf_op jit(solution)/shard_map/scatter | solution.py:118
  180.3 13.1 all-to-all-start.2
  194.0 2.4 all_gather.3
  196.4 2.9 fusion.12
  199.3 462.3 %fusion = f32[16,768]{1,0:T(8,128)} fusion(f32[1536,768]{1,0:T(8,128)} %fusion.12), kind=kCustom, calls=%all-reduce-scatter | all-reduce-scatter fusion | flops 1572865 | bytes 4768768
  665.0 1.3 collective-permute-start.29
  666.3 1.3 collective-permute-start.28
  667.6 1.3 collective-permute-start.27
  671.6 1.3 collective-permute-start.25
  672.9 5.3 collective-permute-done.29
  678.2 1.3 collective-permute-start.24
  679.5 5.8 collective-permute-done.28
  685.3 1.3 collective-permute-start.23
  686.6 2.1 collective-permute-done.27
  690.0 4.7 collective-permute-done.26
  695.9 1.6 collective-permute-done.25
  698.8 3.3 collective-permute-done.24
  702.0 1.3 collective-permute-start.19
  703.3 7.4 collective-permute-done.23
  712.0 5.6 collective-permute-done.22
  718.8 8.3 collective-permute-done.21
  728.5 2.2 collective-permute-done.20
  731.9 2.5 collective-permute-done.19
  736.6 2.2 collective-permute-start.13
  738.8 2.6 collective-permute-start.12
  741.4 2.7 collective-permute-start.11
  744.1 1.9 collective-permute-start.10
  747.8 2.3 reduce.27
  751.0 1.9 collective-permute-start.9
  753.0 1.9 collective-permute-start.8
  754.9 1.9 collective-permute-start.7
  756.9 1.9 collective-permute-start.6
  758.8 1.9 collective-permute-start.5
  760.8 4.3 multiply_reduce_fusion
  765.2 672.5 %psum.31 = f32[7,768]{1,0:T(8,128)S(1)} all-reduce(f32[7,768]{1,0:T(8,128)S(1)} %stack.31), channel_id=1, replica_groups=mesh['dp'=128,'group'=2] {'dp'}, use_global_device_ids=true, to_apply=%region_20.21 | all-reduce | flops 5376 | bytes 43008 | tf_op jit(solution)/shard_map/psum | solution.py:145
  1437.7 15.9 %collective-permute-start.4 = (f32[16,768]{1,0:T(8,128)}, f32[16,768]{1,0:T(8,128)S(1)}, u32[]{:S(2)}, u32[]{:S(2)}) collective-permute-start(f32[16,768]{1,0:T(8,128)} %fusion), channel_id=1, source_target_pairs={{0,10},{2,12},{4,14},{6,16},{8,18},{10,20},{12,22},{14,24},{16,26}... | collective-permute-start | bytes 147464
  1453.6 15.1 collective-permute-start.3
  1468.8 13.4 collective-permute-start.2
  1482.2 8.8 collective-permute-start.1
  1491.0 2.1 collective-permute-start
  1493.8 3.4 collective-permute-done
  1497.2 48.4 %concatenate.4 = f32[524,768]{1,0:T(8,128)} concatenate(f32[12,768]{1,0:T(8,128)} %copy-done.9, f32[16,768]{1,0:T(8,128)} %collective-permute-done.30, f32[16,768]{1,0:T(8,128)} %collective-permute-done.29, f32[16,768]{1,0:T(8,128)} %collective-permute-done.28, f32[16,768]{1,0:T(8,128)} %collective-permute-done.27, f32[16,768]{1,0:T(8,128)} %collective-permute-done.26, ...), dimensions={0} | concatenate | bytes 3219456
  1545.7 1.5 dynamic-slice_multiply_fusion
  1547.2 5.4 copy.27
  1552.6 2.2 fusion.16
  1554.8 1.8 slice_add_fusion
  (108 shorter events, 30.2 us)
Async XLA Ops:
  7.2 46.9 %copy-start = (bf16[1536,768]{1,0:T(8,128)(2,1)S(1)}, bf16[1536,768]{1,0:T(8,128)(2,1)}, u32[]{:S(2)}) copy-start(bf16[1536,768]{1,0:T(8,128)(2,1)} %param.9) | copy-start | bytes 7077892
  33.0 4.0 copy-start.8
  40.5 11.9 copy-start.6
  40.5 12.0 copy-start.10
  40.5 81.8 %all-to-all-start.1 = ((bf16[128,2,8,768]{3,2,1,0:T(8,128)(2,1)}), bf16[128,2,8,768]{3,2,1,0:T(8,128)(2,1)}, u32[]{:S(2)}, u32[]{:S(2)}) async-start(bf16[128,2,8,768]{3,2,1,0:T(8,128)(2,1)} %select_select_fusion), calls=%async_computation.2 | async-start | bytes 6291456 | tf_op jit(solution)/shard_map/all_to_all | solution.py:79
  52.4 19.1 %reduce-scatter.4.cloned.1.call-start = ((), (), s32[]{:S(2)}) async-start(), calls=%async_computation.4 | async-start | bytes 2359296 | tf_op jit(solution)/shard_map/reduce_scatter | solution.py:56
  52.5 0.9 copy-start.4
  54.0 2.0 copy-start.11
  122.2 6.5 copy-start.1
  122.2 6.5 copy-start.12
  148.9 5.8 copy-start.2
  155.2 1.7 copy-start.3
  180.3 13.2 copy-start.5
  180.3 1366.9 %all-to-all-start.2 = ((f32[128,2,8,768]{3,2,1,0:T(8,128)}), f32[128,2,8,768]{3,2,1,0:T(8,128)}, u32[]{:S(2)}, u32[]{:S(2)}) async-start(f32[128,2,8,768]{3,2,1,0:T(8,128)} %bitcast.63), calls=%async_computation.3 | async-start | bytes 12582912 | tf_op jit(solution)/shard_map/all_to_all | solution.py:119
  199.3 546.7 %copy-start.13 = (u32[256]{0:T(256)S(1)}, u32[256]{0:T(256)}, u32[]{:S(2)}) copy-start(u32[256]{0:T(256)} %constant.94) | copy-start | bytes 3076
  199.3 561.4 %copy-start.7 = (bf16[1,256,768]{2,1,0:T(8,128)(2,1)S(1)}, bf16[1,256,768]{2,1,0:T(8,128)(2,1)}, u32[]{:S(2)}) copy-start(bf16[1,256,768]{2,1,0:T(8,128)(2,1)} %param.7) | copy-start | bytes 1179652
  661.6 10.0 collective-permute-start.30
  663.7 6.0 collective-permute-start.31
  665.0 13.2 collective-permute-start.29
  666.3 19.0 %collective-permute-start.28 = (f32[16,768]{1,0:T(8,128)}, f32[16,768]{1,0:T(8,128)}, u32[]{:S(2)}, u32[]{:S(2)}) collective-permute-start(f32[16,768]{1,0:T(8,128)} %fusion), channel_id=1, source_target_pairs={{0,58},{2,60},{4,62},{6,64},{8,66},{10,68},{12,70},{14,72},{16,74}... | collective-permute-start | bytes 147464
  667.6 21.1 %collective-permute-start.27 = (f32[16,768]{1,0:T(8,128)}, f32[16,768]{1,0:T(8,128)}, u32[]{:S(2)}, u32[]{:S(2)}) collective-permute-start(f32[16,768]{1,0:T(8,128)} %fusion), channel_id=1, source_target_pairs={{0,56},{2,58},{4,60},{6,62},{8,64},{10,66},{12,68},{14,70},{16,72}... | collective-permute-start | bytes 147464
  669.7 0.6 copy-start.9
  670.3 24.3 %collective-permute-start.26 = (f32[16,768]{1,0:T(8,128)}, f32[16,768]{1,0:T(8,128)}, u32[]{:S(2)}, u32[]{:S(2)}) collective-permute-start(f32[16,768]{1,0:T(8,128)} %fusion), channel_id=1, source_target_pairs={{0,54},{2,56},{4,58},{6,60},{8,62},{10,64},{12,66},{14,68},{16,70}... | collective-permute-start | bytes 147464
  671.6 25.9 %collective-permute-start.25 = (f32[16,768]{1,0:T(8,128)}, f32[16,768]{1,0:T(8,128)}, u32[]{:S(2)}, u32[]{:S(2)}) collective-permute-start(f32[16,768]{1,0:T(8,128)} %fusion), channel_id=1, source_target_pairs={{0,52},{2,54},{4,56},{6,58},{8,60},{10,62},{12,64},{14,66},{16,68}... | collective-permute-start | bytes 147464
  678.2 23.8 %collective-permute-start.24 = (f32[16,768]{1,0:T(8,128)}, f32[16,768]{1,0:T(8,128)}, u32[]{:S(2)}, u32[]{:S(2)}) collective-permute-start(f32[16,768]{1,0:T(8,128)} %fusion), channel_id=1, source_target_pairs={{0,50},{2,52},{4,54},{6,56},{8,58},{10,60},{12,62},{14,64},{16,66}... | collective-permute-start | bytes 147464
  685.3 25.4 %collective-permute-start.23 = (f32[16,768]{1,0:T(8,128)}, f32[16,768]{1,0:T(8,128)}, u32[]{:S(2)}, u32[]{:S(2)}) collective-permute-start(f32[16,768]{1,0:T(8,128)} %fusion), channel_id=1, source_target_pairs={{0,48},{2,50},{4,52},{6,54},{8,56},{10,58},{12,60},{14,62},{16,64}... | collective-permute-start | bytes 147464
  688.7 28.9 %collective-permute-start.22 = (f32[16,768]{1,0:T(8,128)}, f32[16,768]{1,0:T(8,128)}, u32[]{:S(2)}, u32[]{:S(2)}) collective-permute-start(f32[16,768]{1,0:T(8,128)} %fusion), channel_id=1, source_target_pairs={{0,46},{2,48},{4,50},{6,52},{8,54},{10,56},{12,58},{14,60},{16,62}... | collective-permute-start | bytes 147464
  694.6 32.6 %collective-permute-start.21 = (f32[16,768]{1,0:T(8,128)}, f32[16,768]{1,0:T(8,128)}, u32[]{:S(2)}, u32[]{:S(2)}) collective-permute-start(f32[16,768]{1,0:T(8,128)} %fusion), channel_id=1, source_target_pairs={{0,44},{2,46},{4,48},{6,50},{8,52},{10,54},{12,56},{14,58},{16,60}... | collective-permute-start | bytes 147464
  697.5 33.2 %collective-permute-start.20 = (f32[16,768]{1,0:T(8,128)}, f32[16,768]{1,0:T(8,128)}, u32[]{:S(2)}, u32[]{:S(2)}) collective-permute-start(f32[16,768]{1,0:T(8,128)} %fusion), channel_id=1, source_target_pairs={{0,42},{2,44},{4,46},{6,48},{8,50},{10,52},{12,54},{14,56},{16,58}... | collective-permute-start | bytes 147464
  702.0 32.4 %collective-permute-start.19 = (f32[16,768]{1,0:T(8,128)}, f32[16,768]{1,0:T(8,128)}, u32[]{:S(2)}, u32[]{:S(2)}) collective-permute-start(f32[16,768]{1,0:T(8,128)} %fusion), channel_id=1, source_target_pairs={{0,40},{2,42},{4,44},{6,46},{8,48},{10,50},{12,52},{14,54},{16,56}... | collective-permute-start | bytes 147464
  710.7 25.9 %collective-permute-start.18 = (f32[16,768]{1,0:T(8,128)}, f32[16,768]{1,0:T(8,128)}, u32[]{:S(2)}, u32[]{:S(2)}) collective-permute-start(f32[16,768]{1,0:T(8,128)} %fusion), channel_id=1, source_target_pairs={{0,38},{2,40},{4,42},{6,44},{8,46},{10,48},{12,50},{14,52},{16,54}... | collective-permute-start | bytes 147464
  717.6 21.2 %collective-permute-start.17 = (f32[16,768]{1,0:T(8,128)}, f32[16,768]{1,0:T(8,128)}, u32[]{:S(2)}, u32[]{:S(2)}) collective-permute-start(f32[16,768]{1,0:T(8,128)} %fusion), channel_id=1, source_target_pairs={{0,36},{2,38},{4,40},{6,42},{8,44},{10,46},{12,48},{14,50},{16,52}... | collective-permute-start | bytes 147464
  727.2 14.2 collective-permute-start.16
  730.7 13.4 collective-permute-start.15
  734.5 16.6 %collective-permute-start.14 = (f32[16,768]{1,0:T(8,128)}, f32[16,768]{1,0:T(8,128)}, u32[]{:S(2)}, u32[]{:S(2)}) collective-permute-start(f32[16,768]{1,0:T(8,128)} %fusion), channel_id=1, source_target_pairs={{0,30},{2,32},{4,34},{6,36},{8,38},{10,40},{12,42},{14,44},{16,46}... | collective-permute-start | bytes 147464
  736.6 16.4 %collective-permute-start.13 = (f32[16,768]{1,0:T(8,128)}, f32[16,768]{1,0:T(8,128)}, u32[]{:S(2)}, u32[]{:S(2)}) collective-permute-start(f32[16,768]{1,0:T(8,128)} %fusion), channel_id=1, source_target_pairs={{0,28},{2,30},{4,32},{6,34},{8,36},{10,38},{12,40},{14,42},{16,44}... | collective-permute-start | bytes 147464
  738.8 16.1 %collective-permute-start.12 = (f32[16,768]{1,0:T(8,128)}, f32[16,768]{1,0:T(8,128)}, u32[]{:S(2)}, u32[]{:S(2)}) collective-permute-start(f32[16,768]{1,0:T(8,128)} %fusion), channel_id=1, source_target_pairs={{0,26},{2,28},{4,30},{6,32},{8,34},{10,36},{12,38},{14,40},{16,42}... | collective-permute-start | bytes 147464
  741.4 15.4 collective-permute-start.11
  744.1 14.7 collective-permute-start.10
  751.0 686.6 %collective-permute-start.9 = (f32[16,768]{1,0:T(8,128)}, f32[16,768]{1,0:T(8,128)}, u32[]{:S(2)}, u32[]{:S(2)}) collective-permute-start(f32[16,768]{1,0:T(8,128)} %fusion), channel_id=1, source_target_pairs={{0,20},{2,22},{4,24},{6,26},{8,28},{10,30},{12,32},{14,34},{16,36}... | collective-permute-start | bytes 147464
  753.0 700.6 %collective-permute-start.8 = (f32[16,768]{1,0:T(8,128)}, f32[16,768]{1,0:T(8,128)}, u32[]{:S(2)}, u32[]{:S(2)}) collective-permute-start(f32[16,768]{1,0:T(8,128)} %fusion), channel_id=1, source_target_pairs={{0,18},{2,20},{4,22},{6,24},{8,26},{10,28},{12,30},{14,32},{16,34}... | collective-permute-start | bytes 147464
  754.9 713.8 %collective-permute-start.7 = (f32[16,768]{1,0:T(8,128)}, f32[16,768]{1,0:T(8,128)}, u32[]{:S(2)}, u32[]{:S(2)}) collective-permute-start(f32[16,768]{1,0:T(8,128)} %fusion), channel_id=1, source_target_pairs={{0,16},{2,18},{4,20},{6,22},{8,24},{10,26},{12,28},{14,30},{16,32}... | collective-permute-start | bytes 147464
  756.9 725.3 %collective-permute-start.6 = (f32[16,768]{1,0:T(8,128)}, f32[16,768]{1,0:T(8,128)}, u32[]{:S(2)}, u32[]{:S(2)}) collective-permute-start(f32[16,768]{1,0:T(8,128)} %fusion), channel_id=1, source_target_pairs={{0,14},{2,16},{4,18},{6,20},{8,22},{10,24},{12,26},{14,28},{16,30}... | collective-permute-start | bytes 147464
  758.8 732.2 %collective-permute-start.5 = (f32[16,768]{1,0:T(8,128)}, f32[16,768]{1,0:T(8,128)}, u32[]{:S(2)}, u32[]{:S(2)}) collective-permute-start(f32[16,768]{1,0:T(8,128)} %fusion), channel_id=1, source_target_pairs={{0,12},{2,14},{4,16},{6,18},{8,20},{10,22},{12,24},{14,26},{16,28}... | collective-permute-start | bytes 147464
  1437.7 56.1 %collective-permute-start.4 = (f32[16,768]{1,0:T(8,128)}, f32[16,768]{1,0:T(8,128)S(1)}, u32[]{:S(2)}, u32[]{:S(2)}) collective-permute-start(f32[16,768]{1,0:T(8,128)} %fusion), channel_id=1, source_target_pairs={{0,10},{2,12},{4,14},{6,16},{8,18},{10,20},{12,22},{14,24},{16,26}... | collective-permute-start | bytes 147464
  1453.6 40.2 %collective-permute-start.3 = (f32[16,768]{1,0:T(8,128)}, f32[16,768]{1,0:T(8,128)S(1)}, u32[]{:S(2)}, u32[]{:S(2)}) collective-permute-start(f32[16,768]{1,0:T(8,128)} %fusion), channel_id=1, source_target_pairs={{0,8},{2,10},{4,12},{6,14},{8,16},{10,18},{12,20},{14,22},{16,24},... | collective-permute-start | bytes 147464
  1468.8 25.0 %collective-permute-start.2 = (f32[16,768]{1,0:T(8,128)}, f32[16,768]{1,0:T(8,128)S(1)}, u32[]{:S(2)}, u32[]{:S(2)}) collective-permute-start(f32[16,768]{1,0:T(8,128)} %fusion), channel_id=1, source_target_pairs={{0,6},{2,8},{4,10},{6,12},{8,14},{10,16},{12,18},{14,20},{16,22},{... | collective-permute-start | bytes 147464
  1482.2 11.6 collective-permute-start.1
  1491.0 6.2 collective-permute-start
Sparse Core Ops, SparseCore 0:
  56.2 15.2 reduce-scatter.3
where the time goes:
time: 1570 us; the launch traced here: 1560 us
  blocking collectives  1160 us (74%)
  starting transfers between devices  123 us (8%)
  waiting for transfers between devices  118 us (8%)
  local copies, waits for them, and re-layouts  102 us (6%)
  other arithmetic  24.1 us (2%)
  matrix products  16.6 us (1%)
  between operations  16.2 us (1%)
    psum x1, blocking collectives, per_device(): kernel_grad = lax.psum(kernel_part, 'dp') / device_count  672 us
    unnamed x1, blocking collectives  462 us
    unnamed x32, starting transfers between devices  97.5 us
    unnamed x32, local copies, waits for them, and re-layouts  58.4 us
    unnamed x33, waiting for transfers between devices  53.8 us
    all_to_all x1, waiting for transfers between devices, per_device(): lax.all_to_all(served.reshape(device_count, CAP, ROWS, half_width), 'dp',...  48.7 us
  transfers between devices with their start and end apart: 35, of which 16 were waited for; matrix products, arithmetic and copies ran while one was open for 34% of the time, Pallas kernels for 0%

commit v1 on v0

--- a/solution.py
+++ b/solution.py
@@ -142,7 +142,7 @@
     kernel_part = kernel_term(
         hidden_grad.reshape(seq_count, seq_length, half_width), padded, dw_kernel.shape[0]
     )
-    kernel_grad = lax.psum(kernel_part, "dp") / device_count
+    kernel_grad = jnp.sum(lax.all_gather(kernel_part, "dp"), axis=0) / device_count
     weight_grad = (
         lax.psum_scatter(
             lax.dot_general(

time: 1570 us -> 895 us (0.57)
  the two profiles are of different devices: /device:TPU:54 before, /device:TPU:8 now
where the time goes in v1:
time: 895 us; the launch traced here: 891 us
  blocking collectives  523 us (58%)
  starting transfers between devices  137 us (15%)
  local copies, waits for them, and re-layouts  102 us (11%)
  waiting for transfers between devices  70.1 us (8%)
  other arithmetic  24.8 us (3%)
  matrix products  16.7 us (2%)
  between operations  16.4 us (2%)
    unnamed x1, blocking collectives  490 us
    unnamed x32, starting transfers between devices  119 us
    unnamed x44, local copies, waits for them, and re-layouts  55.8 us
    all_to_all x1, waiting for transfers between devices, per_device(): lax.all_to_all(served.reshape(device_count, CAP, ROWS, half_width), 'dp',...  51 us
    all_to_all x1, blocking collectives, per_device(): lax.all_to_all(wanted.reshape(device_count, CAP), 'dp', split_axis=0, con...  26.2 us
    scatter x1, local copies, waits for them, and re-layouts, per_device(): jnp.zeros((slot_count, ROWS, half_width), jnp.float32).at[slot_index]  18.4 us
  transfers between devices with their start and end apart: 36, of which 4 were waited for; matrix products, arithmetic and copies ran while one was open for 63% of the time, Pallas kernels for 0%

profile of v1, /device:TPU:8, one launch (start us, length us, event | category | flops | bytes accessed | tf_op | source)
XLA Modules:
  0.0 890.7 jit_solution(12890750195773616874)
XLA Ops:
  10.7 26.2 %all_to_all.16 = s32[128,1,2]{2,1,0:T(1,128)S(1)} all-to-all(s32[128,1,2]{2,1,0:T(1,128)S(1)} %bitcast.67), channel_id=1, replica_groups=mesh['dp'=128,'group'=2] {'dp'}, dimensions={0} | all-to-all | bytes 2048 | tf_op jit(solution)/shard_map/all_to_all | solution.py:72
  37.5 3.4 gather_fusion
  40.9 3.5 select_select_fusion
  44.4 7.9 all-to-all-start.1
  54.0 2.0 fusion.14
  56.2 15.8 %reduce-scatter.4.cloned.1.call-done = f32[256,768]{1,0:T(8,128)} async-done(((f32[256,1536]{1,0:T(8,128)}), f32[256,768]{1,0:T(8,128)}) %reduce-scatter.4.cloned.1.call-update) | async-done | bytes 786448 | tf_op jit(solution)/shard_map/reduce_scatter | solution.py:56
  72.0 1.5 fusion.10
  74.0 51.0 %all-to-all-done.1 = bf16[128,2,8,768]{3,2,1,0:T(8,128)(2,1)} async-done(((bf16[128,2,8,768]{3,2,1,0:T(8,128)(2,1)}), bf16[128,2,8,768]{3,2,1,0:T(8,128)(2,1)}, u32[]{:S(2)}, u32[]{:S(2)}) %all-to-all-start.1) | async-done | bytes 3145760 | tf_op jit(solution)/shard_map/all_to_all | solution.py:79
  125.0 3.7 gather_fusion.1
  128.7 2.8 bitcast_select_fusion
  131.5 10.8 %concatenate.3 = bf16[1153,768]{1,0:T(8,128)(2,1)} concatenate(bf16[1,768]{1,0:T(2,128)(2,1)S(1)} %copy-done.18, bf16[128,768]{1,0:T(8,128)(2,1)S(1)} %copy-done.1, bf16[1024,768]{1,0:T(8,128)(2,1)} %bitcast_select_fusion), dimensions={0} | concatenate | bytes 3542016 | tf_op jit(solution)/shard_map/concatenate | solution.py:89
  142.4 1.9 fusion.1
  144.3 3.0 fusion.27
  147.3 4.5 all-reduce.3
  154.5 2.3 convolution_reduce_fusion
  158.0 1.7 copy-done.3
  159.8 1.9 slice_bitcast_fusion
  161.6 3.1 broadcast_in_dim.66
  164.7 18.4 %scatter_fusion = f32[256,8,768]{2,1,0:T(8,128)} fusion(f32[256,8,768]{2,1,0:T(8,128)} %broadcast_in_dim.66, s32[128]{0:T(128)S(1)} %get-tuple-element.37, f32[128,8,768]{2,1,0:T(8,128)} %slice_bitcast_fusion), kind=kCustom, calls=%fused_computation.2 | custom fusion | bytes 9437696 | tf_op jit(solution)/shard_map/scatter | solution.py:118
  183.1 10.3 %all-to-all-start.2 = ((f32[128,2,8,768]{3,2,1,0:T(8,128)}), f32[128,2,8,768]{3,2,1,0:T(8,128)}, u32[]{:S(2)}, u32[]{:S(2)}) async-start(f32[128,2,8,768]{3,2,1,0:T(8,128)} %bitcast.64), calls=%async_computation.3 | async-start | bytes 12582912 | tf_op jit(solution)/shard_map/all_to_all | solution.py:119
  194.0 2.4 all_gather.9
  196.3 4.4 multiply_reduce_fusion
  202.5 1.3 stack.31
  203.9 2.9 fusion.12
  206.8 490.5 %fusion = f32[16,768]{1,0:T(8,128)S(1)} fusion(f32[1536,768]{1,0:T(8,128)} %fusion.12), kind=kCustom, calls=%all-reduce-scatter | all-reduce-scatter fusion | flops 1572865 | bytes 4768768
  697.3 1.3 collective-permute-start.30
  698.6 1.3 collective-permute-start.31
  699.9 1.3 collective-permute-start.29
  701.2 1.3 collective-permute-start.28
  702.5 31.5 %collective-permute-start.27 = (f32[16,768]{1,0:T(8,128)S(1)}, f32[16,768]{1,0:T(8,128)S(1)}, u32[]{:S(2)}, u32[]{:S(2)}) collective-permute-start(f32[16,768]{1,0:T(8,128)S(1)} %fusion), channel_id=1, source_target_pairs={{0,56},{2,58},{4,60},{6,62},{8,64},{10,66},{12,68},{14,70},{16,72}... | collective-permute-start | bytes 147464
  734.0 1.3 collective-permute-start.26
  735.3 1.3 collective-permute-start.25
  736.6 1.3 collective-permute-start.24
  737.9 1.3 collective-permute-start.23
  739.2 1.3 collective-permute-start.22
  740.5 1.3 collective-permute-start.21
  741.9 7.2 collective-permute-start.20
  749.1 5.4 collective-permute-start.19
  754.5 4.2 collective-permute-start.18
  758.7 1.3 collective-permute-start.17
  760.0 4.8 collective-permute-start.16
  764.9 1.3 collective-permute-start.15
  766.2 2.0 collective-permute-start.14
  768.2 3.2 collective-permute-start.13
  771.4 4.6 collective-permute-start.12
  776.0 4.1 collective-permute-start.11
  780.2 2.2 collective-permute-start.10
  782.4 4.4 collective-permute-start.9
  786.8 3.2 collective-permute-start.8
  790.0 1.9 collective-permute-start.7
  792.0 3.7 collective-permute-start.6
  795.7 2.8 collective-permute-start.5
  798.5 4.4 collective-permute-start.4
  803.0 3.9 collective-permute-start.3
  806.9 3.2 collective-permute-start.2
  810.1 4.6 collective-permute-start.1
  814.7 2.1 collective-permute-start
  819.7 3.2 collective-permute-done
  822.9 47.2 %concatenate.4 = f32[524,768]{1,0:T(8,128)} concatenate(f32[12,768]{1,0:T(8,128)S(1)} %collective-permute-done.31, f32[16,768]{1,0:T(8,128)S(1)} %collective-permute-done.30, f32[16,768]{1,0:T(8,128)S(1)} %collective-permute-done.29, f32[16,768]{1,0:T(8,128)S(1)} %collective-permute-done.28, f32[16,768]{1,0:T(8,128)S(1)} %collective-permute-done.27, ...), dimensions={0} | concatenate | bytes 3219456
  870.1 1.5 dynamic-slice_multiply_fusion
  871.6 2.2 reduce_sum.162
  874.4 5.4 copy.27
  879.8 2.2 fusion.16
  882.0 1.8 slice_add_fusion
  (123 shorter events, 15.0 us)
Async XLA Ops:
  7.2 46.8 %copy-start = (bf16[1536,768]{1,0:T(8,128)(2,1)S(1)}, bf16[1536,768]{1,0:T(8,128)(2,1)}, u32[]{:S(2)}) copy-start(bf16[1536,768]{1,0:T(8,128)(2,1)} %param.9) | copy-start | bytes 7077892
  36.9 4.0 copy-start.7
  44.3 8.0 copy-start.6
  44.4 8.1 copy-start.16
  44.4 80.7 %all-to-all-start.1 = ((bf16[128,2,8,768]{3,2,1,0:T(8,128)(2,1)}), bf16[128,2,8,768]{3,2,1,0:T(8,128)(2,1)}, u32[]{:S(2)}, u32[]{:S(2)}) async-start(bf16[128,2,8,768]{3,2,1,0:T(8,128)(2,1)} %select_select_fusion), calls=%async_computation.2 | async-start | bytes 6291456 | tf_op jit(solution)/shard_map/all_to_all | solution.py:79
  52.3 19.7 %reduce-scatter.4.cloned.1.call-start = ((), (), s32[]{:S(2)}) async-start(), calls=%async_computation.4 | async-start | bytes 2359296 | tf_op jit(solution)/shard_map/reduce_scatter | solution.py:56
  52.4 0.9 copy-start.4
  54.0 2.0 copy-start.17
  125.0 6.5 copy-start.1
  125.0 6.5 copy-start.18
  151.7 5.8 copy-start.2
  158.0 1.7 copy-start.3
  183.1 10.3 %copy-start.5 = (f32[256,768]{1,0:T(8,128)S(1)}, f32[256,768]{1,0:T(8,128)}, u32[]{:S(2)}) copy-start(f32[256,768]{1,0:T(8,128)} %reduce-scatter.4.cloned.1.call-done) | copy-start | bytes 2359300
  183.1 691.3 %all-to-all-start.2 = ((f32[128,2,8,768]{3,2,1,0:T(8,128)}), f32[128,2,8,768]{3,2,1,0:T(8,128)}, u32[]{:S(2)}, u32[]{:S(2)}) async-start(f32[128,2,8,768]{3,2,1,0:T(8,128)} %bitcast.64), calls=%async_computation.3 | async-start | bytes 12582912 | tf_op jit(solution)/shard_map/all_to_all | solution.py:119
  193.4 678.2 %all-gather.4.cloned.1.call-start = ((), (), s32[]{:S(2)}) async-start(), calls=%async_computation.5 | async-start | bytes 3170304 | tf_op jit(solution)/shard_map/all_gather | solution.py:145
  206.8 610.1 %copy-start.19 = (u32[256]{0:T(256)S(1)}, u32[256]{0:T(256)}, u32[]{:S(2)}) copy-start(u32[256]{0:T(256)} %constant.94) | copy-start | bytes 3076
  206.8 611.9 %copy-start.8 = (s32[128,1,2]{2,1,0:T(1,128)S(1)}, s32[128,1,2]{2,1,0:T(1,128)}, u32[]{:S(2)}) copy-start(s32[128,1,2]{2,1,0:T(1,128)} %copy-done.7) | copy-start | bytes 3076
  697.3 38.0 %collective-permute-start.30 = (f32[16,768]{1,0:T(8,128)S(1)}, f32[16,768]{1,0:T(8,128)S(1)}, u32[]{:S(2)}, u32[]{:S(2)}) collective-permute-start(f32[16,768]{1,0:T(8,128)S(1)} %fusion), channel_id=1, source_target_pairs={{0,62},{2,64},{4,66},{6,68},{8,70},{10,72},{12,74},{14,76},{16,78}... | collective-permute-start | bytes 147464
  698.6 35.4 %collective-permute-start.31 = (f32[12,768]{1,0:T(8,128)S(1)}, f32[12,768]{1,0:T(8,128)S(1)}, u32[]{:S(2)}, u32[]{:S(2)}) collective-permute-start(f32[12,768]{1,0:T(8,128)S(1)} %slice.74), channel_id=1, source_target_pairs={{0,64},{2,66},{4,68},{6,70},{8,72},{10,74},{12,76},{14,78},{16,80}... | collective-permute-start | bytes 110600
  699.9 36.7 %collective-permute-start.29 = (f32[16,768]{1,0:T(8,128)S(1)}, f32[16,768]{1,0:T(8,128)S(1)}, u32[]{:S(2)}, u32[]{:S(2)}) collective-permute-start(f32[16,768]{1,0:T(8,128)S(1)} %fusion), channel_id=1, source_target_pairs={{0,60},{2,62},{4,64},{6,66},{8,68},{10,70},{12,72},{14,74},{16,76}... | collective-permute-start | bytes 147464
  701.2 36.7 %collective-permute-start.28 = (f32[16,768]{1,0:T(8,128)S(1)}, f32[16,768]{1,0:T(8,128)S(1)}, u32[]{:S(2)}, u32[]{:S(2)}) collective-permute-start(f32[16,768]{1,0:T(8,128)S(1)} %fusion), channel_id=1, source_target_pairs={{0,58},{2,60},{4,62},{6,64},{8,66},{10,68},{12,70},{14,72},{16,74}... | collective-permute-start | bytes 147464
  702.5 36.7 %collective-permute-start.27 = (f32[16,768]{1,0:T(8,128)S(1)}, f32[16,768]{1,0:T(8,128)S(1)}, u32[]{:S(2)}, u32[]{:S(2)}) collective-permute-start(f32[16,768]{1,0:T(8,128)S(1)} %fusion), channel_id=1, source_target_pairs={{0,56},{2,58},{4,60},{6,62},{8,64},{10,66},{12,68},{14,70},{16,72}... | collective-permute-start | bytes 147464
  734.0 6.5 collective-permute-start.26
  735.3 6.5 collective-permute-start.25
  736.6 12.4 %collective-permute-start.24 = (f32[16,768]{1,0:T(8,128)S(1)}, f32[16,768]{1,0:T(8,128)S(1)}, u32[]{:S(2)}, u32[]{:S(2)}) collective-permute-start(f32[16,768]{1,0:T(8,128)S(1)} %fusion), channel_id=1, source_target_pairs={{0,50},{2,52},{4,54},{6,56},{8,58},{10,60},{12,62},{14,64},{16,66}... | collective-permute-start | bytes 147464
  737.9 16.6 %collective-permute-start.23 = (f32[16,768]{1,0:T(8,128)S(1)}, f32[16,768]{1,0:T(8,128)S(1)}, u32[]{:S(2)}, u32[]{:S(2)}) collective-permute-start(f32[16,768]{1,0:T(8,128)S(1)} %fusion), channel_id=1, source_target_pairs={{0,48},{2,50},{4,52},{6,54},{8,56},{10,58},{12,60},{14,62},{16,64}... | collective-permute-start | bytes 147464
  739.2 19.5 %collective-permute-start.22 = (f32[16,768]{1,0:T(8,128)S(1)}, f32[16,768]{1,0:T(8,128)S(1)}, u32[]{:S(2)}, u32[]{:S(2)}) collective-permute-start(f32[16,768]{1,0:T(8,128)S(1)} %fusion), channel_id=1, source_target_pairs={{0,46},{2,48},{4,50},{6,52},{8,54},{10,56},{12,58},{14,60},{16,62}... | collective-permute-start | bytes 147464
  740.5 19.5 %collective-permute-start.21 = (f32[16,768]{1,0:T(8,128)S(1)}, f32[16,768]{1,0:T(8,128)S(1)}, u32[]{:S(2)}, u32[]{:S(2)}) collective-permute-start(f32[16,768]{1,0:T(8,128)S(1)} %fusion), channel_id=1, source_target_pairs={{0,44},{2,46},{4,48},{6,50},{8,52},{10,54},{12,56},{14,58},{16,60}... | collective-permute-start | bytes 147464
  741.9 23.0 %collective-permute-start.20 = (f32[16,768]{1,0:T(8,128)S(1)}, f32[16,768]{1,0:T(8,128)S(1)}, u32[]{:S(2)}, u32[]{:S(2)}) collective-permute-start(f32[16,768]{1,0:T(8,128)S(1)} %fusion), channel_id=1, source_target_pairs={{0,42},{2,44},{4,46},{6,48},{8,50},{10,52},{12,54},{14,56},{16,58}... | collective-permute-start | bytes 147464
  749.1 17.1 %collective-permute-start.19 = (f32[16,768]{1,0:T(8,128)S(1)}, f32[16,768]{1,0:T(8,128)S(1)}, u32[]{:S(2)}, u32[]{:S(2)}) collective-permute-start(f32[16,768]{1,0:T(8,128)S(1)} %fusion), channel_id=1, source_target_pairs={{0,40},{2,42},{4,44},{6,46},{8,48},{10,50},{12,52},{14,54},{16,56}... | collective-permute-start | bytes 147464
  754.5 13.7 %collective-permute-start.18 = (f32[16,768]{1,0:T(8,128)S(1)}, f32[16,768]{1,0:T(8,128)S(1)}, u32[]{:S(2)}, u32[]{:S(2)}) collective-permute-start(f32[16,768]{1,0:T(8,128)S(1)} %fusion), channel_id=1, source_target_pairs={{0,38},{2,40},{4,42},{6,44},{8,46},{10,48},{12,50},{14,52},{16,54}... | collective-permute-start | bytes 147464
  758.7 12.7 %collective-permute-start.17 = (f32[16,768]{1,0:T(8,128)S(1)}, f32[16,768]{1,0:T(8,128)S(1)}, u32[]{:S(2)}, u32[]{:S(2)}) collective-permute-start(f32[16,768]{1,0:T(8,128)S(1)} %fusion), channel_id=1, source_target_pairs={{0,36},{2,38},{4,40},{6,42},{8,44},{10,46},{12,48},{14,50},{16,52}... | collective-permute-start | bytes 147464
  760.0 16.0 %collective-permute-start.16 = (f32[16,768]{1,0:T(8,128)S(1)}, f32[16,768]{1,0:T(8,128)S(1)}, u32[]{:S(2)}, u32[]{:S(2)}) collective-permute-start(f32[16,768]{1,0:T(8,128)S(1)} %fusion), channel_id=1, source_target_pairs={{0,34},{2,36},{4,38},{6,40},{8,42},{10,44},{12,46},{14,48},{16,50}... | collective-permute-start | bytes 147464
  764.9 15.3 %collective-permute-start.15 = (f32[16,768]{1,0:T(8,128)S(1)}, f32[16,768]{1,0:T(8,128)S(1)}, u32[]{:S(2)}, u32[]{:S(2)}) collective-permute-start(f32[16,768]{1,0:T(8,128)S(1)} %fusion), channel_id=1, source_target_pairs={{0,32},{2,34},{4,36},{6,38},{8,40},{10,42},{12,44},{14,46},{16,48}... | collective-permute-start | bytes 147464
  766.2 16.2 %collective-permute-start.14 = (f32[16,768]{1,0:T(8,128)S(1)}, f32[16,768]{1,0:T(8,128)S(1)}, u32[]{:S(2)}, u32[]{:S(2)}) collective-permute-start(f32[16,768]{1,0:T(8,128)S(1)} %fusion), channel_id=1, source_target_pairs={{0,30},{2,32},{4,34},{6,36},{8,38},{10,40},{12,42},{14,44},{16,46}... | collective-permute-start | bytes 147464
  768.2 18.6 %collective-permute-start.13 = (f32[16,768]{1,0:T(8,128)S(1)}, f32[16,768]{1,0:T(8,128)S(1)}, u32[]{:S(2)}, u32[]{:S(2)}) collective-permute-start(f32[16,768]{1,0:T(8,128)S(1)} %fusion), channel_id=1, source_target_pairs={{0,28},{2,30},{4,32},{6,34},{8,36},{10,38},{12,40},{14,42},{16,44}... | collective-permute-start | bytes 147464
  771.4 18.6 %collective-permute-start.12 = (f32[16,768]{1,0:T(8,128)S(1)}, f32[16,768]{1,0:T(8,128)S(1)}, u32[]{:S(2)}, u32[]{:S(2)}) collective-permute-start(f32[16,768]{1,0:T(8,128)S(1)} %fusion), channel_id=1, source_target_pairs={{0,26},{2,28},{4,30},{6,32},{8,34},{10,36},{12,38},{14,40},{16,42}... | collective-permute-start | bytes 147464
  776.0 15.9 %collective-permute-start.11 = (f32[16,768]{1,0:T(8,128)S(1)}, f32[16,768]{1,0:T(8,128)S(1)}, u32[]{:S(2)}, u32[]{:S(2)}) collective-permute-start(f32[16,768]{1,0:T(8,128)S(1)} %fusion), channel_id=1, source_target_pairs={{0,24},{2,26},{4,28},{6,30},{8,32},{10,34},{12,36},{14,38},{16,40}... | collective-permute-start | bytes 147464
  780.2 15.5 %collective-permute-start.10 = (f32[16,768]{1,0:T(8,128)S(1)}, f32[16,768]{1,0:T(8,128)S(1)}, u32[]{:S(2)}, u32[]{:S(2)}) collective-permute-start(f32[16,768]{1,0:T(8,128)S(1)} %fusion), channel_id=1, source_target_pairs={{0,22},{2,24},{4,26},{6,28},{8,30},{10,32},{12,34},{14,36},{16,38}... | collective-permute-start | bytes 147464
  782.4 16.1 %collective-permute-start.9 = (f32[16,768]{1,0:T(8,128)S(1)}, f32[16,768]{1,0:T(8,128)S(1)}, u32[]{:S(2)}, u32[]{:S(2)}) collective-permute-start(f32[16,768]{1,0:T(8,128)S(1)} %fusion), channel_id=1, source_target_pairs={{0,20},{2,22},{4,24},{6,26},{8,28},{10,30},{12,32},{14,34},{16,36}... | collective-permute-start | bytes 147464
  786.8 16.1 %collective-permute-start.8 = (f32[16,768]{1,0:T(8,128)S(1)}, f32[16,768]{1,0:T(8,128)S(1)}, u32[]{:S(2)}, u32[]{:S(2)}) collective-permute-start(f32[16,768]{1,0:T(8,128)S(1)} %fusion), channel_id=1, source_target_pairs={{0,18},{2,20},{4,22},{6,24},{8,26},{10,28},{12,30},{14,32},{16,34}... | collective-permute-start | bytes 147464
  790.0 16.8 %collective-permute-start.7 = (f32[16,768]{1,0:T(8,128)S(1)}, f32[16,768]{1,0:T(8,128)S(1)}, u32[]{:S(2)}, u32[]{:S(2)}) collective-permute-start(f32[16,768]{1,0:T(8,128)S(1)} %fusion), channel_id=1, source_target_pairs={{0,16},{2,18},{4,20},{6,22},{8,24},{10,26},{12,28},{14,30},{16,32}... | collective-permute-start | bytes 147464
  791.9 26.2 %copy-start.9 = (f32[16,768]{1,0:T(8,128)}, f32[16,768]{1,0:T(8,128)S(1)}, u32[]{:S(2)}) copy-start(f32[16,768]{1,0:T(8,128)S(1)} %collective-permute-done.11) | copy-start | bytes 147460
  792.0 18.1 %collective-permute-start.6 = (f32[16,768]{1,0:T(8,128)S(1)}, f32[16,768]{1,0:T(8,128)S(1)}, u32[]{:S(2)}, u32[]{:S(2)}) collective-permute-start(f32[16,768]{1,0:T(8,128)S(1)} %fusion), channel_id=1, source_target_pairs={{0,14},{2,16},{4,18},{6,20},{8,22},{10,24},{12,26},{14,28},{16,30}... | collective-permute-start | bytes 147464
  795.7 19.0 %copy-start.10 = (f32[16,768]{1,0:T(8,128)}, f32[16,768]{1,0:T(8,128)S(1)}, u32[]{:S(2)}) copy-start(f32[16,768]{1,0:T(8,128)S(1)} %collective-permute-done.10) | copy-start | bytes 147460
  795.7 19.0 %collective-permute-start.5 = (f32[16,768]{1,0:T(8,128)S(1)}, f32[16,768]{1,0:T(8,128)S(1)}, u32[]{:S(2)}, u32[]{:S(2)}) collective-permute-start(f32[16,768]{1,0:T(8,128)S(1)} %fusion), channel_id=1, source_target_pairs={{0,12},{2,14},{4,16},{6,18},{8,20},{10,22},{12,24},{14,26},{16,28}... | collective-permute-start | bytes 147464
  798.5 18.4 %copy-start.11 = (f32[16,768]{1,0:T(8,128)}, f32[16,768]{1,0:T(8,128)S(1)}, u32[]{:S(2)}) copy-start(f32[16,768]{1,0:T(8,128)S(1)} %collective-permute-done.9) | copy-start | bytes 147460
  798.5 21.1 %collective-permute-start.4 = (f32[16,768]{1,0:T(8,128)S(1)}, f32[16,768]{1,0:T(8,128)}, u32[]{:S(2)}, u32[]{:S(2)}) collective-permute-start(f32[16,768]{1,0:T(8,128)S(1)} %fusion), channel_id=1, source_target_pairs={{0,10},{2,12},{4,14},{6,16},{8,18},{10,20},{12,22},{14,24},{16,26}... | collective-permute-start | bytes 147464
  802.9 13.9 %copy-start.12 = (f32[16,768]{1,0:T(8,128)}, f32[16,768]{1,0:T(8,128)S(1)}, u32[]{:S(2)}) copy-start(f32[16,768]{1,0:T(8,128)S(1)} %collective-permute-done.8) | copy-start | bytes 147460
  803.0 16.7 %collective-permute-start.3 = (f32[16,768]{1,0:T(8,128)S(1)}, f32[16,768]{1,0:T(8,128)}, u32[]{:S(2)}, u32[]{:S(2)}) collective-permute-start(f32[16,768]{1,0:T(8,128)S(1)} %fusion), channel_id=1, source_target_pairs={{0,8},{2,10},{4,12},{6,14},{8,16},{10,18},{12,20},{14,22},{16,24},... | collective-permute-start | bytes 147464
  806.8 10.1 %copy-start.13 = (f32[16,768]{1,0:T(8,128)}, f32[16,768]{1,0:T(8,128)S(1)}, u32[]{:S(2)}) copy-start(f32[16,768]{1,0:T(8,128)S(1)} %collective-permute-done.7) | copy-start | bytes 147460
  806.9 12.8 %collective-permute-start.2 = (f32[16,768]{1,0:T(8,128)S(1)}, f32[16,768]{1,0:T(8,128)}, u32[]{:S(2)}, u32[]{:S(2)}) collective-permute-start(f32[16,768]{1,0:T(8,128)S(1)} %fusion), channel_id=1, source_target_pairs={{0,6},{2,8},{4,10},{6,12},{8,14},{10,16},{12,18},{14,20},{16,22},{... | collective-permute-start | bytes 147464
  810.1 6.8 copy-start.14
  810.1 9.6 %collective-permute-start.1 = (f32[16,768]{1,0:T(8,128)S(1)}, f32[16,768]{1,0:T(8,128)}, u32[]{:S(2)}, u32[]{:S(2)}) collective-permute-start(f32[16,768]{1,0:T(8,128)S(1)} %fusion), channel_id=1, source_target_pairs={{0,4},{2,6},{4,8},{6,10},{8,12},{10,14},{12,16},{14,18},{16,20},{1... | collective-permute-start | bytes 147464
  814.7 2.2 copy-start.15
  814.7 8.2 collective-permute-start
Sparse Core Ops, SparseCore 0:
  56.1 15.8 reduce-scatter.3
  204.0 139.2 all-gather.3
